TPU v7x, 32 devices: a whole 2x2x4 slice. The times are simulated.
32 devices in a mesh: gx: 4 (over z), gy: 4 (over x, core), ha: 2 (over y).
Axes of the slice: x: 2, y: 2, z: 4, core: 2. Of those that a mesh axis runs over, the one named last changes fastest.
Arguments:
- offsets: float32 [3, 8, 8, 4, 128], P(None, 'gx', 'gy', 'ha'), may hold values from 0 to 1
- forces: float32 [3, 8, 8, 4, 128], P(None, 'gx', 'gy', 'ha'), may hold values from -6 to 6
- counts: int32 [8, 8, 4], P('gx', 'gy', 'ha'), may hold values from 16 to 128, as said below
Outputs:
- velocity: float32 [3, 8, 8, 4, 128], P(None, 'gx', 'gy', 'ha')
Inputs may be any that keep to these rules, and one draw needn't show every extreme that they name: `counts`: A bin is heavy when its count exceeds 64. The 16 bins that two devices differing only in their ha index hold together include at most 8 heavy bins; in every draw some such pair holds exactly 8, all on one device; some bin holds exactly 128.
All inputs are finite; a program needn't handle non-finite values.
Results may differ from a plain program's by a relative error of at most 0.0003.
Values sent between devices are 32-bit elements; how exact they have to be, the bound alone decides.
No kernel may reach another device: no remote copies, remote signals or barrier semaphores. Data moves between devices by JAX's collectives and lax.ppermute only.
A program may use at most 64 MiB of HBM per device.

v0:
```python
import math

import jax
import jax.numpy as jnp
from jax import lax
from jax.sharding import PartitionSpec as P

SPLIT_XI = 2.0
SOFT_SQ = 0.01
GAUSS_COEF = 2.0 * SPLIT_XI / math.sqrt(math.pi)
STOKES_NORM = 1.0 / (8.0 * math.pi)


def padded(array, sides, width):
    for axis, dim in sides:
        size, length = (lax.axis_size(axis), array.shape[dim])
        up = [(i, (i + 1) % size) for i in range(size)]
        down = [(j, i) for i, j in up]
        last = lax.slice_in_dim(array, length - width, length, axis=dim)
        initial = lax.slice_in_dim(array, 0, width, axis=dim)
        before = lax.ppermute(last, axis, up)
        after = lax.ppermute(initial, axis, down)
        array = jnp.concatenate([before, array, after], axis=dim)
    return array


def pair_kernel(targets, row_ids, source_data, capacity):
    n_source = source_data.shape[1]
    flat_ids = jnp.arange(n_source, dtype=jnp.int32)
    neighbour = flat_ids // capacity
    step_x = (neighbour // 9 - 1).astype(jnp.float32)
    step_y = (neighbour // 3 % 3 - 1).astype(jnp.float32)
    step_z = (neighbour % 3 - 1).astype(jnp.float32)
    delta_x = targets[0][:, None] - (source_data[0] + step_x)[None, :]
    delta_y = targets[1][:, None] - (source_data[1] + step_y)[None, :]
    delta_z = targets[2][:, None] - (source_data[2] + step_z)[None, :]
    square = delta_x * delta_x + delta_y * delta_y + delta_z * delta_z + SOFT_SQ
    radius = jnp.sqrt(square)
    tail_erfc = jax.scipy.special.erfc(SPLIT_XI * radius)
    gaussian = jnp.exp(-SPLIT_XI * SPLIT_XI * square)
    coef_c = tail_erfc / radius + GAUSS_COEF * (2.0 * SPLIT_XI * SPLIT_XI * square - 3.0) * gaussian
    coef_d = (
        tail_erfc / radius + GAUSS_COEF * (1.0 - 2.0 * SPLIT_XI * SPLIT_XI * square) * gaussian
    ) / square
    keep_pair = flat_ids[None, :] != 13 * capacity + row_ids[:, None]
    coef_c = jnp.where(keep_pair, coef_c, 0.0)
    coef_d = jnp.where(keep_pair, coef_d, 0.0)
    force_x = source_data[3][None, :]
    force_y = source_data[4][None, :]
    force_z = source_data[5][None, :]
    along_d = coef_d * (delta_x * force_x + delta_y * force_y + delta_z * force_z)
    vel_x = jnp.sum(coef_c * force_x + along_d * delta_x, axis=1)
    vel_y = jnp.sum(coef_c * force_y + along_d * delta_y, axis=1)
    vel_z = jnp.sum(coef_c * force_z + along_d * delta_z, axis=1)
    return STOKES_NORM * jnp.stack([vel_x, vel_y, vel_z])


def on_device(offsets, forces, counts):
    capacity = offsets.shape[4]
    half_rows = capacity // 2
    size_x = offsets.shape[1]
    size_y = offsets.shape[2]
    size_z = offsets.shape[3]
    n_bins = size_x * size_y * size_z
    my_index = lax.axis_index("ha")
    slot_ids = jnp.arange(capacity, dtype=jnp.int32)
    live_mask = (slot_ids[None, None, None, :] < counts[..., None]).astype(jnp.float32)
    packed = jnp.concatenate([offsets, forces * live_mask[None]], axis=0)
    extended = padded(packed, (("gx", 1), ("gy", 2), ("ha", 3)), 1)
    padded_cells = jnp.concatenate(
        [extended[:, :, :, -1:], extended, extended[:, :, :, :1]], axis=3
    )
    zero_index = jnp.zeros((), jnp.int32)

    def center_of(flat_id, owner_index):
        bin_x = flat_id // (size_y * size_z)
        bin_y = flat_id // size_z % size_y
        bin_z = flat_id % size_z
        ext_z = (size_z * owner_index + bin_z - size_z * my_index + 1) % (2 * size_z)
        return (bin_x + 1, bin_y + 1, ext_z)

    def fetch_data(center_x, center_y, center_z):
        start_x = center_x - 1
        start_y = center_y - 1
        start_z = jnp.asarray(center_z)
        window = lax.dynamic_slice(
            padded_cells,
            (zero_index, start_x, start_y, start_z, zero_index),
            (6, 3, 3, 3, capacity),
        )
        return window.reshape(6, 27 * capacity)

    def fetch_own(flat_id):
        center_x, center_y, center_z = center_of(flat_id, my_index)
        return fetch_data(center_x, center_y, center_z)

    first_rows = slot_ids[:half_rows]
    second_rows = slot_ids[half_rows:]

    def first_unit(flat_id):
        source_data = fetch_own(flat_id)
        lower = source_data[0:3, 13 * capacity : 13 * capacity + half_rows]
        return pair_kernel(lower, first_rows, source_data, capacity)

    def second_from(source_data):
        upper = source_data[0:3, 13 * capacity + half_rows : 14 * capacity]
        return pair_kernel(upper, second_rows, source_data, capacity)

    bin_ids = jnp.arange(n_bins, dtype=jnp.int32)
    first_part = lax.map(first_unit, bin_ids)
    heavy_flag = (counts.reshape(-1) > half_rows).astype(jnp.int32)
    n_heavy = jnp.sum(heavy_flag)
    ranked = jnp.argsort((1 - heavy_flag) * n_bins + bin_ids)
    placed = jnp.zeros((n_bins, 3, half_rows), jnp.float32)

    def owner_unit(flat_id):
        return second_from(fetch_own(flat_id))

    second_part = lax.map(owner_unit, ranked)
    rank_valid = (bin_ids < n_heavy).astype(jnp.float32)
    placed = placed.at[ranked].add(second_part * rank_valid[:, None, None])
    merged = jnp.concatenate([first_part, placed], axis=2)
    result = merged.reshape(size_x, size_y, size_z, 3, capacity).transpose(3, 0, 1, 2, 4)
    return result * live_mask[None]


def solution(mesh):
    in_specs = (
        P(None, "gx", "gy", "ha", None),
        P(None, "gx", "gy", "ha", None),
        P("gx", "gy", "ha"),
    )
    out_specs = P(None, "gx", "gy", "ha", None)
    return jax.shard_map(
        on_device, mesh=mesh, in_specs=in_specs, out_specs=out_specs, check_vma=False
    )
```

profile of v0, /device:TPU:0, one launch (start us, length us, event | category | flops | bytes accessed | tf_op | source)
XLA Modules:
  0.0 137.6 jit_solution(15474040716072390123)
XLA Ops:
  1.5 3.1 %collective-permute-start = (f32[6,1,2,2,128]{4,3,2,1,0:T(2,128)S(1)}, f32[6,1,2,2,128]{4,3,2,1,0:T(2,128)S(1)}, u32[]{:S(2)}, u32[]{:S(2)}) collective-permute-start(f32[6,1,2,2,128]{4,3,2,1,0:T(2,128)S(1)} %get-tuple-element.441), channel_id=1, source_target_pairs={{0,8},{8,16},{16,24},{24,0},{1,9},{9,17},{17,25},{25,1},{2,10},{10... | collective-permute-start | bytes 36872 | tf_op jit(solution)/shard_map/ppermute | solution.py:21
  4.6 2.1 %collective-permute-start.1 = (f32[6,1,2,2,128]{4,3,2,1,0:T(2,128)S(1)}, f32[6,1,2,2,128]{4,3,2,1,0:T(2,128)S(1)}, u32[]{:S(2)}, u32[]{:S(2)}) collective-permute-start(f32[6,1,2,2,128]{4,3,2,1,0:T(2,128)S(1)} %get-tuple-element.442), channel_id=1, source_target_pairs={{8,0},{16,8},{24,16},{0,24},{9,1},{17,9},{25,17},{1,25},{10,2},{18... | collective-permute-start | bytes 36872 | tf_op jit(solution)/shard_map/ppermute | solution.py:22
  8.6 1.7 %collective-permute-start.3 = (f32[6,4,1,2,128]{4,3,2,1,0:T(2,128)S(1)}, f32[6,4,1,2,128]{4,3,2,1,0:T(2,128)S(1)}, u32[]{:S(2)}, u32[]{:S(2)}) collective-permute-start(f32[6,4,1,2,128]{4,3,2,1,0:T(2,128)S(1)} %get-tuple-element.440), channel_id=1, source_target_pairs={{2,0},{4,2},{6,4},{0,6},{3,1},{5,3},{7,5},{1,7},{10,8},{12,10},{14... | collective-permute-start | bytes 73736 | tf_op jit(solution)/shard_map/ppermute | solution.py:22
  10.3 1.5 %collective-permute-done.2 = f32[6,4,1,2,128]{4,3,2,1,0:T(2,128)S(1)} collective-permute-done((f32[6,4,1,2,128]{4,3,2,1,0:T(2,128)S(1)}, f32[6,4,1,2,128]{4,3,2,1,0:T(2,128)S(1)}, u32[]{:S(2)}, u32[]{:S(2)}) %collective-permute-start.2) | collective-permute-done | bytes 24608 | tf_op jit(solution)/shard_map/ppermute | solution.py:21
  12.0 1.7 %collective-permute-start.4 = (f32[6,4,4,1,128]{4,3,2,1,0:T(1,128)S(1)}, f32[6,4,4,1,128]{4,3,2,1,0:T(1,128)S(1)}, u32[]{:S(2)}, u32[]{:S(2)}) collective-permute-start(f32[6,4,4,1,128]{4,3,2,1,0:T(1,128)S(1)} %get-tuple-element.438), channel_id=1, source_target_pairs={{1,0},{0,1},{3,2},{2,3},{5,4},{4,5},{7,6},{6,7},{9,8},{8,9},{11,10... | collective-permute-start | bytes 147464 | tf_op jit(solution)/shard_map/ppermute | solution.py:22
  16.1 1.9 %collective-permute-done.5 = f32[6,4,4,1,128]{4,3,2,1,0:T(1,128)S(1)} collective-permute-done((f32[6,4,4,1,128]{4,3,2,1,0:T(1,128)S(1)}, f32[6,4,4,1,128]{4,3,2,1,0:T(1,128)S(1)}, u32[]{:S(2)}, u32[]{:S(2)}) %collective-permute-start.5) | collective-permute-done | bytes 49184 | tf_op jit(solution)/shard_map/ppermute | solution.py:21
  18.4 57.5 %while.35 = (s32[]{:T(128)}, f32[8,3,64]{2,1,0:T(4,128)S(1)}, s32[64]{0:T(128)S(1)}, s32[8]{0:T(128)S(1)}, f32[6,4,4,6,128]{4,3,2,1,0:T(8,128)S(1)}, /*index=5*/...) while((s32[]{:T(128)}, f32[8,3,64]{2,1,0:T(4,128)S(1)}, ...), condition=%wide.region_10.11_spmd.clone, body=%wide.region_6.10_spmd.clone.sunk | while | flops 22958724 | bytes 837763 | solution.py:119
  21.7 3.9 %fusion.112 = (f32[64]{0:T(128)S(1)}, f32[64]{0:T(128)S(1)}, f32[64]{0:T(128)S(1)}) fusion(f32[3456]{0:T(1024)S(1)} %mul.1384, f32[3456]{0:T(1024)S(1)} %get-tuple-element.552, f32[64]{0:T(128)S(1)} %get-tuple-element.553, f32[3456]{0:T(1024)S(1)} %fusion.111, f32[64]{0:T(128)S(1)} %get-tuple-element.555, f32[3456]{0:T(1024)S(1)} %get-tuple-element.556, ...), kind=kLoop, calls=%fused_computation.108.clone.1 | loop fusion | flops 22781760 | bytes 84736 | tf_op jit(solution)/shard_map/while/body/eval_jaxpr/reduce_sum | solution.py:52
  28.9 3.9 %fusion.112 = (f32[64]{0:T(128)S(1)}, f32[64]{0:T(128)S(1)}, f32[64]{0:T(128)S(1)}) fusion(f32[3456]{0:T(1024)S(1)} %mul.1384, f32[3456]{0:T(1024)S(1)} %get-tuple-element.552, f32[64]{0:T(128)S(1)} %get-tuple-element.553, f32[3456]{0:T(1024)S(1)} %fusion.111, f32[64]{0:T(128)S(1)} %get-tuple-element.555, f32[3456]{0:T(1024)S(1)} %get-tuple-element.556, ...), kind=kLoop, calls=%fused_computation.108.clone.1 | loop fusion | flops 22781760 | bytes 84736 | tf_op jit(solution)/shard_map/while/body/eval_jaxpr/reduce_sum | solution.py:52
  36.1 3.9 %fusion.112 = (f32[64]{0:T(128)S(1)}, f32[64]{0:T(128)S(1)}, f32[64]{0:T(128)S(1)}) fusion(f32[3456]{0:T(1024)S(1)} %mul.1384, f32[3456]{0:T(1024)S(1)} %get-tuple-element.552, f32[64]{0:T(128)S(1)} %get-tuple-element.553, f32[3456]{0:T(1024)S(1)} %fusion.111, f32[64]{0:T(128)S(1)} %get-tuple-element.555, f32[3456]{0:T(1024)S(1)} %get-tuple-element.556, ...), kind=kLoop, calls=%fused_computation.108.clone.1 | loop fusion | flops 22781760 | bytes 84736 | tf_op jit(solution)/shard_map/while/body/eval_jaxpr/reduce_sum | solution.py:52
  43.3 3.9 %fusion.112 = (f32[64]{0:T(128)S(1)}, f32[64]{0:T(128)S(1)}, f32[64]{0:T(128)S(1)}) fusion(f32[3456]{0:T(1024)S(1)} %mul.1384, f32[3456]{0:T(1024)S(1)} %get-tuple-element.552, f32[64]{0:T(128)S(1)} %get-tuple-element.553, f32[3456]{0:T(1024)S(1)} %fusion.111, f32[64]{0:T(128)S(1)} %get-tuple-element.555, f32[3456]{0:T(1024)S(1)} %get-tuple-element.556, ...), kind=kLoop, calls=%fused_computation.108.clone.1 | loop fusion | flops 22781760 | bytes 84736 | tf_op jit(solution)/shard_map/while/body/eval_jaxpr/reduce_sum | solution.py:52
  50.5 3.9 %fusion.112 = (f32[64]{0:T(128)S(1)}, f32[64]{0:T(128)S(1)}, f32[64]{0:T(128)S(1)}) fusion(f32[3456]{0:T(1024)S(1)} %mul.1384, f32[3456]{0:T(1024)S(1)} %get-tuple-element.552, f32[64]{0:T(128)S(1)} %get-tuple-element.553, f32[3456]{0:T(1024)S(1)} %fusion.111, f32[64]{0:T(128)S(1)} %get-tuple-element.555, f32[3456]{0:T(1024)S(1)} %get-tuple-element.556, ...), kind=kLoop, calls=%fused_computation.108.clone.1 | loop fusion | flops 22781760 | bytes 84736 | tf_op jit(solution)/shard_map/while/body/eval_jaxpr/reduce_sum | solution.py:52
  57.7 3.9 %fusion.112 = (f32[64]{0:T(128)S(1)}, f32[64]{0:T(128)S(1)}, f32[64]{0:T(128)S(1)}) fusion(f32[3456]{0:T(1024)S(1)} %mul.1384, f32[3456]{0:T(1024)S(1)} %get-tuple-element.552, f32[64]{0:T(128)S(1)} %get-tuple-element.553, f32[3456]{0:T(1024)S(1)} %fusion.111, f32[64]{0:T(128)S(1)} %get-tuple-element.555, f32[3456]{0:T(1024)S(1)} %get-tuple-element.556, ...), kind=kLoop, calls=%fused_computation.108.clone.1 | loop fusion | flops 22781760 | bytes 84736 | tf_op jit(solution)/shard_map/while/body/eval_jaxpr/reduce_sum | solution.py:52
  64.9 3.9 %fusion.112 = (f32[64]{0:T(128)S(1)}, f32[64]{0:T(128)S(1)}, f32[64]{0:T(128)S(1)}) fusion(f32[3456]{0:T(1024)S(1)} %mul.1384, f32[3456]{0:T(1024)S(1)} %get-tuple-element.552, f32[64]{0:T(128)S(1)} %get-tuple-element.553, f32[3456]{0:T(1024)S(1)} %fusion.111, f32[64]{0:T(128)S(1)} %get-tuple-element.555, f32[3456]{0:T(1024)S(1)} %get-tuple-element.556, ...), kind=kLoop, calls=%fused_computation.108.clone.1 | loop fusion | flops 22781760 | bytes 84736 | tf_op jit(solution)/shard_map/while/body/eval_jaxpr/reduce_sum | solution.py:52
  72.0 3.9 %fusion.112 = (f32[64]{0:T(128)S(1)}, f32[64]{0:T(128)S(1)}, f32[64]{0:T(128)S(1)}) fusion(f32[3456]{0:T(1024)S(1)} %mul.1384, f32[3456]{0:T(1024)S(1)} %get-tuple-element.552, f32[64]{0:T(128)S(1)} %get-tuple-element.553, f32[3456]{0:T(1024)S(1)} %fusion.111, f32[64]{0:T(128)S(1)} %get-tuple-element.555, f32[3456]{0:T(1024)S(1)} %get-tuple-element.556, ...), kind=kLoop, calls=%fused_computation.108.clone.1 | loop fusion | flops 22781760 | bytes 84736 | tf_op jit(solution)/shard_map/while/body/eval_jaxpr/reduce_sum | solution.py:52
  76.0 60.0 %while.34 = (s32[]{:T(128)}, f32[8,3,64]{2,1,0:T(4,128)S(1)}, s32[64]{0:T(128)S(1)}, s32[8]{0:T(128)S(1)}, f32[6,4,4,6,128]{4,3,2,1,0:T(8,128)S(1)}, /*index=5*/...) while((s32[]{:T(128)}, f32[8,3,64]{2,1,0:T(4,128)S(1)}, ...), condition=%wide.region_4.5_spmd.clone, body=%wide.region_0.4_spmd.clone.sunk | while | flops 22958724 | bytes 837763 | solution.py:110
  79.6 3.9 %fusion.108 = (f32[64]{0:T(128)S(1)}, f32[64]{0:T(128)S(1)}, f32[64]{0:T(128)S(1)}) fusion(f32[3456]{0:T(1024)S(1)} %mul.1361, f32[3456]{0:T(1024)S(1)} %get-tuple-element.533, f32[64]{0:T(128)S(1)} %get-tuple-element.534, f32[3456]{0:T(1024)S(1)} %fusion.107, f32[64]{0:T(128)S(1)} %get-tuple-element.536, f32[3456]{0:T(1024)S(1)} %get-tuple-element.537, ...), kind=kLoop, calls=%fused_computation.20.clone.1 | loop fusion | flops 22781760 | bytes 84736 | tf_op jit(solution)/shard_map/while/body/eval_jaxpr/reduce_sum | solution.py:52
  87.1 3.9 %fusion.108 = (f32[64]{0:T(128)S(1)}, f32[64]{0:T(128)S(1)}, f32[64]{0:T(128)S(1)}) fusion(f32[3456]{0:T(1024)S(1)} %mul.1361, f32[3456]{0:T(1024)S(1)} %get-tuple-element.533, f32[64]{0:T(128)S(1)} %get-tuple-element.534, f32[3456]{0:T(1024)S(1)} %fusion.107, f32[64]{0:T(128)S(1)} %get-tuple-element.536, f32[3456]{0:T(1024)S(1)} %get-tuple-element.537, ...), kind=kLoop, calls=%fused_computation.20.clone.1 | loop fusion | flops 22781760 | bytes 84736 | tf_op jit(solution)/shard_map/while/body/eval_jaxpr/reduce_sum | solution.py:52
  94.6 3.9 %fusion.108 = (f32[64]{0:T(128)S(1)}, f32[64]{0:T(128)S(1)}, f32[64]{0:T(128)S(1)}) fusion(f32[3456]{0:T(1024)S(1)} %mul.1361, f32[3456]{0:T(1024)S(1)} %get-tuple-element.533, f32[64]{0:T(128)S(1)} %get-tuple-element.534, f32[3456]{0:T(1024)S(1)} %fusion.107, f32[64]{0:T(128)S(1)} %get-tuple-element.536, f32[3456]{0:T(1024)S(1)} %get-tuple-element.537, ...), kind=kLoop, calls=%fused_computation.20.clone.1 | loop fusion | flops 22781760 | bytes 84736 | tf_op jit(solution)/shard_map/while/body/eval_jaxpr/reduce_sum | solution.py:52
  102.1 3.9 %fusion.108 = (f32[64]{0:T(128)S(1)}, f32[64]{0:T(128)S(1)}, f32[64]{0:T(128)S(1)}) fusion(f32[3456]{0:T(1024)S(1)} %mul.1361, f32[3456]{0:T(1024)S(1)} %get-tuple-element.533, f32[64]{0:T(128)S(1)} %get-tuple-element.534, f32[3456]{0:T(1024)S(1)} %fusion.107, f32[64]{0:T(128)S(1)} %get-tuple-element.536, f32[3456]{0:T(1024)S(1)} %get-tuple-element.537, ...), kind=kLoop, calls=%fused_computation.20.clone.1 | loop fusion | flops 22781760 | bytes 84736 | tf_op jit(solution)/shard_map/while/body/eval_jaxpr/reduce_sum | solution.py:52
  109.6 3.9 %fusion.108 = (f32[64]{0:T(128)S(1)}, f32[64]{0:T(128)S(1)}, f32[64]{0:T(128)S(1)}) fusion(f32[3456]{0:T(1024)S(1)} %mul.1361, f32[3456]{0:T(1024)S(1)} %get-tuple-element.533, f32[64]{0:T(128)S(1)} %get-tuple-element.534, f32[3456]{0:T(1024)S(1)} %fusion.107, f32[64]{0:T(128)S(1)} %get-tuple-element.536, f32[3456]{0:T(1024)S(1)} %get-tuple-element.537, ...), kind=kLoop, calls=%fused_computation.20.clone.1 | loop fusion | flops 22781760 | bytes 84736 | tf_op jit(solution)/shard_map/while/body/eval_jaxpr/reduce_sum | solution.py:52
  117.1 3.9 %fusion.108 = (f32[64]{0:T(128)S(1)}, f32[64]{0:T(128)S(1)}, f32[64]{0:T(128)S(1)}) fusion(f32[3456]{0:T(1024)S(1)} %mul.1361, f32[3456]{0:T(1024)S(1)} %get-tuple-element.533, f32[64]{0:T(128)S(1)} %get-tuple-element.534, f32[3456]{0:T(1024)S(1)} %fusion.107, f32[64]{0:T(128)S(1)} %get-tuple-element.536, f32[3456]{0:T(1024)S(1)} %get-tuple-element.537, ...), kind=kLoop, calls=%fused_computation.20.clone.1 | loop fusion | flops 22781760 | bytes 84736 | tf_op jit(solution)/shard_map/while/body/eval_jaxpr/reduce_sum | solution.py:52
  124.6 3.9 %fusion.108 = (f32[64]{0:T(128)S(1)}, f32[64]{0:T(128)S(1)}, f32[64]{0:T(128)S(1)}) fusion(f32[3456]{0:T(1024)S(1)} %mul.1361, f32[3456]{0:T(1024)S(1)} %get-tuple-element.533, f32[64]{0:T(128)S(1)} %get-tuple-element.534, f32[3456]{0:T(1024)S(1)} %fusion.107, f32[64]{0:T(128)S(1)} %get-tuple-element.536, f32[3456]{0:T(1024)S(1)} %get-tuple-element.537, ...), kind=kLoop, calls=%fused_computation.20.clone.1 | loop fusion | flops 22781760 | bytes 84736 | tf_op jit(solution)/shard_map/while/body/eval_jaxpr/reduce_sum | solution.py:52
  132.1 3.9 %fusion.108 = (f32[64]{0:T(128)S(1)}, f32[64]{0:T(128)S(1)}, f32[64]{0:T(128)S(1)}) fusion(f32[3456]{0:T(1024)S(1)} %mul.1361, f32[3456]{0:T(1024)S(1)} %get-tuple-element.533, f32[64]{0:T(128)S(1)} %get-tuple-element.534, f32[3456]{0:T(1024)S(1)} %fusion.107, f32[64]{0:T(128)S(1)} %get-tuple-element.536, f32[3456]{0:T(1024)S(1)} %get-tuple-element.537, ...), kind=kLoop, calls=%fused_computation.20.clone.1 | loop fusion | flops 22781760 | bytes 84736 | tf_op jit(solution)/shard_map/while/body/eval_jaxpr/reduce_sum | solution.py:52
  (277 shorter events, 21.9 us)
Async XLA Ops:
  0.8 0.7 copy-start
  1.5 5.2 %copy-start.1 = (s32[2,2,2]{2,1,0:T(2,128)S(1)}, s32[2,2,2]{2,1,0:T(2,128)}, u32[]{:S(2)}) copy-start(s32[2,2,2]{2,1,0:T(2,128)} %param.9) | copy-start | bytes 100
  1.5 6.9 %collective-permute-start = (f32[6,1,2,2,128]{4,3,2,1,0:T(2,128)S(1)}, f32[6,1,2,2,128]{4,3,2,1,0:T(2,128)S(1)}, u32[]{:S(2)}, u32[]{:S(2)}) collective-permute-start(f32[6,1,2,2,128]{4,3,2,1,0:T(2,128)S(1)} %get-tuple-element.441), channel_id=1, source_target_pairs={{0,8},{8,16},{16,24},{24,0},{1,9},{9,17},{17,25},{25,1},{2,10},{10... | collective-permute-start | bytes 36872 | tf_op jit(solution)/shard_map/ppermute | solution.py:21
  4.6 3.9 %collective-permute-start.1 = (f32[6,1,2,2,128]{4,3,2,1,0:T(2,128)S(1)}, f32[6,1,2,2,128]{4,3,2,1,0:T(2,128)S(1)}, u32[]{:S(2)}, u32[]{:S(2)}) collective-permute-start(f32[6,1,2,2,128]{4,3,2,1,0:T(2,128)S(1)} %get-tuple-element.442), channel_id=1, source_target_pairs={{8,0},{16,8},{24,16},{0,24},{9,1},{17,9},{25,17},{1,25},{10,2},{18... | collective-permute-start | bytes 36872 | tf_op jit(solution)/shard_map/ppermute | solution.py:22
  8.5 3.3 %collective-permute-start.2 = (f32[6,4,1,2,128]{4,3,2,1,0:T(2,128)S(1)}, f32[6,4,1,2,128]{4,3,2,1,0:T(2,128)S(1)}, u32[]{:S(2)}, u32[]{:S(2)}) collective-permute-start(f32[6,4,1,2,128]{4,3,2,1,0:T(2,128)S(1)} %get-tuple-element.439), channel_id=1, source_target_pairs={{0,2},{2,4},{4,6},{6,0},{1,3},{3,5},{5,7},{7,1},{8,10},{10,12},{12... | collective-permute-start | bytes 73736 | tf_op jit(solution)/shard_map/ppermute | solution.py:21
  8.6 3.3 %collective-permute-start.3 = (f32[6,4,1,2,128]{4,3,2,1,0:T(2,128)S(1)}, f32[6,4,1,2,128]{4,3,2,1,0:T(2,128)S(1)}, u32[]{:S(2)}, u32[]{:S(2)}) collective-permute-start(f32[6,4,1,2,128]{4,3,2,1,0:T(2,128)S(1)} %get-tuple-element.440), channel_id=1, source_target_pairs={{2,0},{4,2},{6,4},{0,6},{3,1},{5,3},{7,5},{1,7},{10,8},{12,10},{14... | collective-permute-start | bytes 73736 | tf_op jit(solution)/shard_map/ppermute | solution.py:22
  12.0 4.2 %collective-permute-start.4 = (f32[6,4,4,1,128]{4,3,2,1,0:T(1,128)S(1)}, f32[6,4,4,1,128]{4,3,2,1,0:T(1,128)S(1)}, u32[]{:S(2)}, u32[]{:S(2)}) collective-permute-start(f32[6,4,4,1,128]{4,3,2,1,0:T(1,128)S(1)} %get-tuple-element.438), channel_id=1, source_target_pairs={{1,0},{0,1},{3,2},{2,3},{5,4},{4,5},{7,6},{6,7},{9,8},{8,9},{11,10... | collective-permute-start | bytes 147464 | tf_op jit(solution)/shard_map/ppermute | solution.py:22
  13.7 4.3 %collective-permute-start.5 = (f32[6,4,4,1,128]{4,3,2,1,0:T(1,128)S(1)}, f32[6,4,4,1,128]{4,3,2,1,0:T(1,128)S(1)}, u32[]{:S(2)}, u32[]{:S(2)}) collective-permute-start(f32[6,4,4,1,128]{4,3,2,1,0:T(1,128)S(1)} %get-tuple-element.437), channel_id=1, source_target_pairs={{0,1},{1,0},{2,3},{3,2},{4,5},{5,4},{6,7},{7,6},{8,9},{9,8},{10,11... | collective-permute-start | bytes 147464 | tf_op jit(solution)/shard_map/ppermute | solution.py:21
where the time goes:
time: 138 us
  other arithmetic  68.7 us (50%)
  loops' own time  41.3 us (30%)
  local copies, waits for them, and re-layouts  13.7 us (10%)
  starting transfers between devices  9.05 us (7%)
  waiting for transfers between devices  4.7 us (3%)
    reduce_sum x16, other arithmetic, pair_kernel(): vel_x = jnp.sum(coef_c * force_x + along_d * delta_x, axis=1)  62.2 us
    another operation x1, loops' own time, on_device(): first_part = lax.map(first_unit, bin_ids)  22.1 us
    another operation x1, loops' own time, on_device(): second_part = lax.map(owner_unit, ranked)  19.2 us
    dynamic_slice x16, local copies, waits for them, and re-layouts, on_device(): first_part = lax.map(first_unit, bin_ids)  9.33 us
    ppermute x3, starting transfers between devices, padded(): after = lax.ppermute(initial, axis, down)  5.56 us
    ppermute x3, starting transfers between devices, padded(): before = lax.ppermute(last, axis, up)  3.48 us
    ppermute x3, waiting for transfers between devices, padded(): before = lax.ppermute(last, axis, up)  3.36 us
  transfers between devices with their start and end apart: 6, of which 3 were waited for; matrix products, arithmetic and copies ran while one was open for 2% of the time, Pallas kernels for 0%

commit v1 on v0

v1 whole, which is shorter than its diff:
```python
import functools
import math

import jax
import jax.numpy as jnp
from jax import lax
from jax.experimental import pallas as pl
from jax.experimental.pallas import tpu as pltpu
from jax.sharding import PartitionSpec as P

SPLIT_XI = 2.0
SOFT_SQ = 0.01
GAUSS_COEF = 2.0 * SPLIT_XI / math.sqrt(math.pi)
STOKES_NORM = 1.0 / (8.0 * math.pi)

SOFT_U = SPLIT_XI * SPLIT_XI * SOFT_SQ
LOG2_E = math.log2(math.e)
LOG2_G = math.log2(GAUSS_COEF)
SELF_C = math.erfc(math.sqrt(SOFT_U)) / math.sqrt(SOFT_SQ) + GAUSS_COEF * (
    2.0 * SOFT_U - 3.0
) * math.exp(-SOFT_U)

LANES = 128
ROWS = 8
CHUNK = 32
BLOCK = 2
COUNT_ROW = 6


def assemble(ext, cells, pieces):
    own, other, x_lo, x_hi, y_lo, y_hi = pieces
    row = lax.broadcasted_iota(jnp.int32, (ROWS, LANES), 0)
    lane = lax.broadcasted_iota(jnp.int32, (ROWS, LANES), 1)
    scale = jnp.where(row < 3, SPLIT_XI, 1.0)
    shift = jnp.where(row < 3, -0.5 * SPLIT_XI, 0.0)
    size_x, size_y, size_z = cells
    held = jnp.zeros((ROWS, LANES), jnp.float32)
    for ix in range(size_x + 2):
        for iy in range(size_y + 2):
            for iz in range(2 * size_z):
                if iy == 0:
                    tile = y_lo[ix, 0, iz]
                elif iy == size_y + 1:
                    tile = y_hi[ix, 0, iz]
                elif ix == 0:
                    tile = x_lo[0, iy - 1, iz]
                elif ix == size_x + 1:
                    tile = x_hi[0, iy - 1, iz]
                elif iz < size_z:
                    tile = own[ix - 1, iy - 1, iz]
                else:
                    tile = other[ix - 1, iy - 1, iz - size_z]
                cell = (ix * (size_y + 2) + iy) * 2 * size_z + iz
                ext[cell] = tile * scale + shift
                held = jnp.where(lane == cell, tile, held)
    return held


def pair_block(target, source):
    delta = [target[i] - source[i : i + 1] for i in range(3)]
    force = [source[3 + i : 4 + i] for i in range(3)]
    u = (delta[0] * delta[0] + SOFT_U) + delta[1] * delta[1] + delta[2] * delta[2]
    inv = lax.rsqrt(u)
    tail = (1.0 - lax.erf(u * inv)) * inv
    gauss = jnp.exp2(LOG2_G - u * LOG2_E)
    rest = gauss * (u - 1.5)
    coef_c = tail + rest
    coef_d = ((tail - rest) - gauss) * (inv * inv)
    along = coef_d * (delta[0] * force[0] + delta[1] * force[1] + delta[2] * force[2])
    return [coef_c * force[i] + along * delta[i] for i in range(3)]


def near_kernel(cells, *refs):
    pieces, (out_ref, ext, step_ref, count_v, count_s, sem, listed, spread, summed) = refs[:6], refs[6:]
    size_x, size_y, size_z = cells
    n_z = 2 * size_z
    row = lax.broadcasted_iota(jnp.int32, (ROWS, LANES), 0)
    lane = lax.broadcasted_iota(jnp.int32, (ROWS, LANES), 1)
    zero_tile = jnp.zeros((ROWS, LANES), jnp.float32)

    held = assemble(ext, cells, pieces)
    count_v[...] = held.astype(jnp.int32)
    copy = pltpu.make_async_copy(count_v, count_s, sem)
    copy.start()
    steps = [(0, 0, 0)] + [
        (a, b, c)
        for a in (-1, 0, 1)
        for b in (-1, 0, 1)
        for c in (-1, 0, 1)
        if (a, b, c) != (0, 0, 0)
    ]
    for n, step in enumerate(steps):
        moved = zero_tile
        for i in range(3):
            moved = jnp.where(row == i, SPLIT_XI * step[i], moved)
        step_ref[n] = moved
    copy.wait()

    def one_bin(flat_id, carry):
        bin_x = flat_id // (size_y * size_z)
        bin_y = flat_id // size_z % size_y
        bin_z = flat_id % size_z

        def cell_of(step):
            at_z = lax.rem(bin_z + step[2] + n_z, n_z)
            return ((bin_x + 1 + step[0]) * (size_y + 2) + (bin_y + 1 + step[1])) * n_z + at_z

        current = zero_tile
        filled = jnp.int32(0)
        for n, step in enumerate(steps):
            cell = cell_of(step)
            count = count_s[COUNT_ROW, cell]
            tile_id = lax.shift_right_logical(filled, 7)
            at = lax.bitwise_and(filled, LANES - 1)
            moved = pltpu.roll(ext[cell] + step_ref[n], at, 1)
            behind = lane >= at
            current = jnp.where(behind, moved, current)
            spill = jnp.where(behind, 0.0, moved)
            listed[tile_id] = current
            listed[tile_id + 1] = spill
            filled = filled + count
            current = jnp.where(at + count >= LANES, spill, current)
        last = lax.shift_right_logical(filled, 7)
        for more in range(1, BLOCK):
            listed[last + more] = zero_tile
        n_blocks = lax.div(filled + BLOCK * LANES - 1, BLOCK * LANES)

        own_cell = cell_of((0, 0, 0))
        own_tile = ext[own_cell]
        own_count = count_s[COUNT_ROW, own_cell]
        columns = jnp.transpose(jnp.concatenate([own_tile] * (LANES // ROWS), axis=0))
        for i in range(3):
            spread[i] = jnp.broadcast_to(columns[:, i : i + 1], (LANES, LANES))

        def one_chunk(chunk, carry):
            first = pl.multiple_of(chunk * CHUNK, CHUNK)
            target = [spread[i, pl.ds(first, CHUNK), :] for i in range(3)]

            def one_block(block, sums):
                sums = list(sums)
                for b in range(BLOCK):
                    terms = pair_block(target, listed[block * BLOCK + b])
                    sums = [s + t for s, t in zip(sums, terms)]
                return tuple(sums)

            zero = jnp.zeros((CHUNK, LANES), jnp.float32)
            sums = lax.fori_loop(0, n_blocks, one_block, (zero, zero, zero))
            wide = lax.broadcasted_iota(jnp.int32, (CHUNK, LANES), 1)
            merged = zero
            for i in range(3):
                merged = jnp.where(wide == i, jnp.sum(sums[i], axis=1, keepdims=True), merged)
            summed[pl.ds(first, CHUNK), :] = merged
            return carry

        lax.fori_loop(0, lax.div(own_count + CHUNK - 1, CHUNK), one_chunk, 0)
        result = jnp.transpose(summed[...])[:ROWS]
        slot = lax.broadcasted_iota(jnp.int32, (1, LANES), 1)
        for i in range(3):
            velocity = (2.0 * STOKES_NORM) * result[i : i + 1] - (STOKES_NORM * SELF_C) * own_tile[
                3 + i : 4 + i
            ]
            velocity = jnp.where(slot < own_count, velocity, 0.0)
            out_ref[i, bin_x, bin_y, pl.ds(bin_z, 1), :] = velocity
        return carry

    lax.fori_loop(0, size_x * size_y * size_z, one_bin, 0)


def shifted(array, axis, dim):
    size, length = lax.axis_size(axis), array.shape[dim]
    up = [(i, (i + 1) % size) for i in range(size)]
    down = [(j, i) for i, j in up]
    before = lax.ppermute(lax.slice_in_dim(array, length - 1, length, axis=dim), axis, up)
    after = lax.ppermute(lax.slice_in_dim(array, 0, 1, axis=dim), axis, down)
    return before, after


def on_device(offsets, forces, counts):
    cells = offsets.shape[1:4]
    slots = offsets.shape[4]
    n_cells = (cells[0] + 2) * (cells[1] + 2) * 2 * cells[2]
    live = lax.broadcasted_iota(jnp.int32, cells + (slots,), 3) < counts[..., None]
    spread = jnp.broadcast_to(counts.astype(jnp.float32)[..., None], cells + (slots,))
    rows = [offsets[i] for i in range(3)] + [jnp.where(live, forces[i], 0.0) for i in range(3)]
    rows = rows + [spread, jnp.zeros_like(spread)]
    own = jnp.stack(rows, axis=3)

    size = lax.axis_size("ha")
    other = lax.ppermute(own, "ha", [(i, (i + 1) % size) for i in range(size)])
    column = jnp.concatenate([own, other], axis=2)
    x_lo, x_hi = shifted(column, "gx", 0)
    wide = jnp.concatenate([x_lo, column, x_hi], axis=0)
    y_lo, y_hi = shifted(wide, "gy", 1)

    whole = pl.BlockSpec(memory_space=pltpu.VMEM)
    return pl.pallas_call(
        functools.partial(near_kernel, cells),
        out_shape=jax.ShapeDtypeStruct((3,) + cells + (slots,), jnp.float32),
        in_specs=[whole] * 6,
        out_specs=whole,
        scratch_shapes=[
            pltpu.VMEM((n_cells, ROWS, LANES), jnp.float32),
            pltpu.VMEM((27, ROWS, LANES), jnp.float32),
            pltpu.VMEM((ROWS, LANES), jnp.int32),
            pltpu.SMEM((ROWS, LANES), jnp.int32),
            pltpu.SemaphoreType.DMA,
            pltpu.VMEM((28 + BLOCK, ROWS, LANES), jnp.float32),
            pltpu.VMEM((3, LANES, LANES), jnp.float32),
            pltpu.VMEM((LANES, LANES), jnp.float32),
        ],
        compiler_params=pltpu.CompilerParams(vmem_limit_bytes=16 << 20),
        name="near_field",
    )(own, other, x_lo, x_hi, y_lo, y_hi)


def solution(mesh):
    in_specs = (
        P(None, "gx", "gy", "ha", None),
        P(None, "gx", "gy", "ha", None),
        P("gx", "gy", "ha"),
    )
    out_specs = P(None, "gx", "gy", "ha", None)
    return jax.shard_map(on_device, mesh=mesh, in_specs=in_specs, out_specs=out_specs, check_vma=False)
```

time: 138 us -> 40.3 us (0.29)
  other arithmetic: 68.7 us -> 0.78 us
  loops' own time: 41.3 us -> 0 us
  Pallas kernels: 0 us -> 18.9 us
  local copies, waits for them, and re-layouts: 13.7 us -> 1.56 us
  waiting for transfers between devices: 4.7 us -> 11.5 us
    reduce_sum x17 -> x0, other arithmetic: 62.8 us -> none  [the longest x16 62.2 us: pair_kernel(): vel_x = jnp.sum(coef_c * force_x + along_d * delta_x, axis=1)]
    another operation x2 -> x0, loops' own time: 41.3 us -> none  [the longest x1 22.1 us: on_device(): first_part = lax.map(first_unit, bin_ids)]
    pallas_call x0 -> x1, Pallas kernels: none -> 18.9 us  [on_device(): pl.pallas_call(functools.partial(near_kernel, cells), out_shape=jax.Shape...]
    dynamic_slice x32 -> x0, local copies, waits for them, and re-layouts: 9.94 us -> none  [the longest x16 9.33 us: on_device(): first_part = lax.map(first_unit, bin_ids)]
    ppermute x6 -> x5, waiting for transfers between devices: 4.7 us -> 11.5 us  [the longest x2 6.64 us: shifted(): lax.ppermute(lax.slice_in_dim(array, length - 1, length, axis=dim), axis,...]
    mul x3 -> x0, other arithmetic: 1.41 us -> none  [the longest x1 0.73 us: on_device(): packed = jnp.concatenate([offsets, forces * live_mask[None]], axis=0)]
    ppermute x6 -> x5, starting transfers between devices: 9.05 us -> 7.69 us  [the longest x2 4.16 us: shifted(): after = lax.ppermute(lax.slice_in_dim(array, 0, 1, axis=dim), axis, down)]
  transfers between devices with their start and end apart: 6 -> 5, of which waited for: 3 -> 5; matrix products, arithmetic and copies ran while one was open for 2% -> 0% of each run, Pallas kernels for 0% -> 0%
where the time goes in v1:
time: 40.3 us; the launch traced here: 40.5 us
  Pallas kernels  18.9 us (47%)
  waiting for transfers between devices  11.5 us (29%)
  starting transfers between devices  7.69 us (19%)
  local copies, waits for them, and re-layouts  1.56 us (4%)
  other arithmetic  0.78 us (2%)
    pallas_call x1, Pallas kernels, on_device(): pl.pallas_call(functools.partial(near_kernel, cells), out_shape=jax.Shape...  18.9 us
    ppermute x2, waiting for transfers between devices, shifted(): lax.ppermute(lax.slice_in_dim(array, length - 1, length, axis=dim), axis,...  6.64 us
    ppermute x2, starting transfers between devices, shifted(): after = lax.ppermute(lax.slice_in_dim(array, 0, 1, axis=dim), axis, down)  4.16 us
    ppermute x1, starting transfers between devices, on_device(): other = lax.ppermute(own, 'ha', [(i, (i + 1) % size) for i in range(size)])  3.03 us
    ppermute x2, waiting for transfers between devices, shifted(): after = lax.ppermute(lax.slice_in_dim(array, 0, 1, axis=dim), axis, down)  3 us
    ppermute x1, waiting for transfers between devices, on_device(): other = lax.ppermute(own, 'ha', [(i, (i + 1) % size) for i in range(size)])  1.89 us
  transfers between devices with their start and end apart: 5, of which 5 were waited for; matrix products, arithmetic and copies ran while one was open for 0% of the time, Pallas kernels for 0%

profile of v1, /device:TPU:0, one launch (start us, length us, event | category | flops | bytes accessed | tf_op | source)
XLA Modules:
  0.0 40.5 jit_solution(15898892693553560661)
XLA Ops:
  0.0 0.7 %convert_element_type.3 = f32[2,2,2]{2,1,0:T(2,128)S(1)} convert(s32[2,2,2]{2,1,0:T(2,128)} %param.5) | non-fusion elementwise | flops 8 | bytes 64 | tf_op jit(solution)/shard_map/convert_element_type | solution.py:183
  0.7 0.0 copy-start
  0.7 0.7 %fusion.6 = (f32[1,2,2,2,128]{4,3,2,1,0:T(2,128)S(1)}, f32[1,2,2,2,128]{4,3,2,1,0:T(2,128)S(1)}, f32[1,2,2,2,128]{4,3,2,1,0:T(2,128)S(1)}) fusion(f32[3,2,2,2,128]{4,3,2,1,0:T(2,128)} %param.3), kind=kLoop, calls=%fused_computation.11 | loop fusion | bytes 24576 | tf_op jit(solution)/shard_map/slice | solution.py:184
  1.4 0.0 copy-done
  1.4 0.0 copy-start.1
  1.4 0.7 %copy-done.1 = s32[2,2,2]{2,1,0:T(2,128)S(1)} copy-done((s32[2,2,2]{2,1,0:T(2,128)S(1)}, s32[2,2,2]{2,1,0:T(2,128)}, u32[]{:S(2)}) %copy-start.1) | copy-done | bytes 56
  2.1 0.1 fusion.1
  2.2 0.1 stack_broadcast_in_dim.2
  2.3 0.1 stack.2.refs_0_
  2.3 3.0 %collective-permute-start = (f32[2,2,2,8,128]{4,3,2,1,0:T(8,128)S(1)}, f32[2,2,2,8,128]{4,3,2,1,0:T(8,128)S(1)}, u32[]{:S(2)}, u32[]{:S(2)}) collective-permute-start(f32[2,2,2,8,128]{4,3,2,1,0:T(8,128)S(1)} %stack.2.refs_0_), channel_id=1, source_target_pairs={{0,1},{1,0},{2,3},{3,2},{4,5},{5,4},{6,7},{7,6},{8,9},{9,8},{10,11... | collective-permute-start | bytes 98312 | tf_op jit(solution)/shard_map/ppermute | solution.py:189
  5.4 1.9 %collective-permute-done.refs_1_ = f32[2,2,2,8,128]{4,3,2,1,0:T(8,128)S(1)} collective-permute-done((f32[2,2,2,8,128]{4,3,2,1,0:T(8,128)S(1)}, f32[2,2,2,8,128]{4,3,2,1,0:T(8,128)S(1)}, u32[]{:S(2)}, u32[]{:S(2)}) %collective-permute-start) | collective-permute-done | bytes 32800 | tf_op jit(solution)/shard_map/ppermute | solution.py:189
  7.3 4.1 %collective-permute-start.2 = (f32[1,2,4,8,128]{4,3,2,1,0:T(8,128)S(1)}, f32[1,2,4,8,128]{4,3,2,1,0:T(8,128)S(1)}, u32[]{:S(2)}, u32[]{:S(2)}) collective-permute-start(f32[1,2,4,8,128]{4,3,2,1,0:T(8,128)S(1)} %get-tuple-element.7), channel_id=1, source_target_pairs={{8,0},{16,8},{24,16},{0,24},{9,1},{17,9},{25,17},{1,25},{10,2},{18... | collective-permute-start | bytes 98312 | tf_op jit(solution)/shard_map/ppermute | solution.py:174
  11.4 0.0 collective-permute-start.1
  11.4 1.6 %collective-permute-done.2.refs_3_ = f32[1,2,4,8,128]{4,3,2,1,0:T(8,128)S(1)} collective-permute-done((f32[1,2,4,8,128]{4,3,2,1,0:T(8,128)S(1)}, f32[1,2,4,8,128]{4,3,2,1,0:T(8,128)S(1)}, u32[]{:S(2)}, u32[]{:S(2)}) %collective-permute-start.2) | collective-permute-done | bytes 32800 | tf_op jit(solution)/shard_map/ppermute | solution.py:174
  13.0 4.1 %collective-permute-done.1.refs_2_ = f32[1,2,4,8,128]{4,3,2,1,0:T(8,128)S(1)} collective-permute-done((f32[1,2,4,8,128]{4,3,2,1,0:T(8,128)S(1)}, f32[1,2,4,8,128]{4,3,2,1,0:T(8,128)S(1)}, u32[]{:S(2)}, u32[]{:S(2)}) %collective-permute-start.1) | collective-permute-done | bytes 32800 | tf_op jit(solution)/shard_map/ppermute | solution.py:173
  17.1 0.1 collective-permute-start.4
  17.2 0.5 %collective-permute-start.3 = (f32[4,1,4,8,128]{4,3,2,1,0:T(8,128)S(1)}, f32[4,1,4,8,128]{4,3,2,1,0:T(8,128)S(1)}, u32[]{:S(2)}, u32[]{:S(2)}) collective-permute-start(f32[4,1,4,8,128]{4,3,2,1,0:T(8,128)S(1)} %get-tuple-element.6), channel_id=1, source_target_pairs={{0,2},{2,4},{4,6},{6,0},{1,3},{3,5},{5,7},{7,1},{8,10},{10,12},{12... | collective-permute-start | bytes 196616 | tf_op jit(solution)/shard_map/ppermute | solution.py:173
  17.7 1.4 %collective-permute-done.4.refs_5_ = f32[4,1,4,8,128]{4,3,2,1,0:T(8,128)S(1)} collective-permute-done((f32[4,1,4,8,128]{4,3,2,1,0:T(8,128)S(1)}, f32[4,1,4,8,128]{4,3,2,1,0:T(8,128)S(1)}, u32[]{:S(2)}, u32[]{:S(2)}) %collective-permute-start.4) | collective-permute-done | bytes 65568 | tf_op jit(solution)/shard_map/ppermute | solution.py:174
  19.1 2.5 %collective-permute-done.3.refs_4_ = f32[4,1,4,8,128]{4,3,2,1,0:T(8,128)S(1)} collective-permute-done((f32[4,1,4,8,128]{4,3,2,1,0:T(8,128)S(1)}, f32[4,1,4,8,128]{4,3,2,1,0:T(8,128)S(1)}, u32[]{:S(2)}, u32[]{:S(2)}) %collective-permute-start.3) | collective-permute-done | bytes 65568 | tf_op jit(solution)/shard_map/ppermute | solution.py:173
  21.6 18.9 %near_field.1 = f32[3,2,2,2,128]{4,3,2,1,0:T(2,128)} custom-call(f32[2,2,2,8,128]{4,3,2,1,0:T(8,128)S(1)} %stack.2.refs_0_, f32[2,2,2,8,128]{4,3,2,1,0:T(8,128)S(1)} %collective-permute-done.refs_1_, f32[1,2,4,8,128]{4,3,2,1,0:T(8,128)S(1)} %collective-permute-done.1.refs_2_, f32[1,2,4,8,128]{4,3,2,1,0:T(8,128)S(1)} %collective-permute-done.2.refs_3_, ...), custom_call_target="tpu_custom_call" | custom-call | tf_op jit(solution)/shard_map/near_field/pallas_call | solution.py:196
  (5 shorter events, 0.0 us)
Async XLA Ops:
  0.7 0.7 %copy-start = (f32[3,2,2,2,128]{4,3,2,1,0:T(2,128)S(1)}, f32[3,2,2,2,128]{4,3,2,1,0:T(2,128)}, u32[]{:S(2)}) copy-start(f32[3,2,2,2,128]{4,3,2,1,0:T(2,128)} %param.4) | copy-start | bytes 36868
  1.4 0.7 %copy-start.1 = (s32[2,2,2]{2,1,0:T(2,128)S(1)}, s32[2,2,2]{2,1,0:T(2,128)}, u32[]{:S(2)}) copy-start(s32[2,2,2]{2,1,0:T(2,128)} %param.5) | copy-start | bytes 100
  2.3 4.9 %collective-permute-start = (f32[2,2,2,8,128]{4,3,2,1,0:T(8,128)S(1)}, f32[2,2,2,8,128]{4,3,2,1,0:T(8,128)S(1)}, u32[]{:S(2)}, u32[]{:S(2)}) collective-permute-start(f32[2,2,2,8,128]{4,3,2,1,0:T(8,128)S(1)} %stack.2.refs_0_), channel_id=1, source_target_pairs={{0,1},{1,0},{2,3},{3,2},{4,5},{5,4},{6,7},{7,6},{8,9},{9,8},{10,11... | collective-permute-start | bytes 98312 | tf_op jit(solution)/shard_map/ppermute | solution.py:189
  7.3 5.7 %collective-permute-start.2 = (f32[1,2,4,8,128]{4,3,2,1,0:T(8,128)S(1)}, f32[1,2,4,8,128]{4,3,2,1,0:T(8,128)S(1)}, u32[]{:S(2)}, u32[]{:S(2)}) collective-permute-start(f32[1,2,4,8,128]{4,3,2,1,0:T(8,128)S(1)} %get-tuple-element.7), channel_id=1, source_target_pairs={{8,0},{16,8},{24,16},{0,24},{9,1},{17,9},{25,17},{1,25},{10,2},{18... | collective-permute-start | bytes 98312 | tf_op jit(solution)/shard_map/ppermute | solution.py:174
  11.4 5.7 %collective-permute-start.1 = (f32[1,2,4,8,128]{4,3,2,1,0:T(8,128)S(1)}, f32[1,2,4,8,128]{4,3,2,1,0:T(8,128)S(1)}, u32[]{:S(2)}, u32[]{:S(2)}) collective-permute-start(f32[1,2,4,8,128]{4,3,2,1,0:T(8,128)S(1)} %get-tuple-element.8), channel_id=1, source_target_pairs={{0,8},{8,16},{16,24},{24,0},{1,9},{9,17},{17,25},{25,1},{2,10},{10... | collective-permute-start | bytes 98312 | tf_op jit(solution)/shard_map/ppermute | solution.py:173
  17.1 2.0 %collective-permute-start.4 = (f32[4,1,4,8,128]{4,3,2,1,0:T(8,128)S(1)}, f32[4,1,4,8,128]{4,3,2,1,0:T(8,128)S(1)}, u32[]{:S(2)}, u32[]{:S(2)}) collective-permute-start(f32[4,1,4,8,128]{4,3,2,1,0:T(8,128)S(1)} %get-tuple-element.5), channel_id=1, source_target_pairs={{2,0},{4,2},{6,4},{0,6},{3,1},{5,3},{7,5},{1,7},{10,8},{12,10},{14... | collective-permute-start | bytes 196616 | tf_op jit(solution)/shard_map/ppermute | solution.py:174
  17.2 4.4 %collective-permute-start.3 = (f32[4,1,4,8,128]{4,3,2,1,0:T(8,128)S(1)}, f32[4,1,4,8,128]{4,3,2,1,0:T(8,128)S(1)}, u32[]{:S(2)}, u32[]{:S(2)}) collective-permute-start(f32[4,1,4,8,128]{4,3,2,1,0:T(8,128)S(1)} %get-tuple-element.6), channel_id=1, source_target_pairs={{0,2},{2,4},{4,6},{6,0},{1,3},{3,5},{5,7},{7,1},{8,10},{10,12},{12... | collective-permute-start | bytes 196616 | tf_op jit(solution)/shard_map/ppermute | solution.py:173

commit v2 on v1

--- a/solution.py
+++ b/solution.py
@@ -27,31 +27,48 @@
 COUNT_ROW = 6
 
 
+def pack_kernel(cells, count_ref, offset_ref, force_ref, out_ref):
+    slot = lax.broadcasted_iota(jnp.int32, (1, LANES), 1)
+    for ix in range(cells[0]):
+        for iy in range(cells[1]):
+            for iz in range(cells[2]):
+                count = count_ref[ix, iy, iz]
+                for i in range(3):
+                    position = offset_ref[i, ix, iy, iz : iz + 1, :]
+                    out_ref[ix, iy, iz, i : i + 1, :] = position * SPLIT_XI - 0.5 * SPLIT_XI
+                    force = force_ref[i, ix, iy, iz : iz + 1, :]
+                    out_ref[ix, iy, iz, 3 + i : 4 + i, :] = jnp.where(slot < count, force, 0.0)
+                out_ref[ix, iy, iz, 6:8, :] = jnp.full((2, LANES), count, jnp.int32).astype(jnp.float32)
+
+
+def window_kernel(cells, n_y, at_ref, gathered_ref, out_ref):
+    size_x, size_y, size_z = cells
+    gy, ha = at_ref[0], at_ref[1]
+    for iy in range(size_y + 2):
+        from_y = lax.rem(gy * size_y + iy - 1 + n_y, n_y)
+        for iz in range(2 * size_z):
+            from_ha = ha if iz < size_z else 1 - ha
+            device = 2 * lax.div(from_y, size_y) + from_ha
+            for ix in range(size_x):
+                out_ref[ix, iy, iz] = gathered_ref[device, ix, lax.rem(from_y, size_y), iz % size_z]
+
+
 def assemble(ext, cells, pieces):
-    own, other, x_lo, x_hi, y_lo, y_hi = pieces
-    row = lax.broadcasted_iota(jnp.int32, (ROWS, LANES), 0)
+    inner, x_lo, x_hi = pieces
     lane = lax.broadcasted_iota(jnp.int32, (ROWS, LANES), 1)
-    scale = jnp.where(row < 3, SPLIT_XI, 1.0)
-    shift = jnp.where(row < 3, -0.5 * SPLIT_XI, 0.0)
     size_x, size_y, size_z = cells
     held = jnp.zeros((ROWS, LANES), jnp.float32)
     for ix in range(size_x + 2):
         for iy in range(size_y + 2):
             for iz in range(2 * size_z):
-                if iy == 0:
-                    tile = y_lo[ix, 0, iz]
-                elif iy == size_y + 1:
-                    tile = y_hi[ix, 0, iz]
-                elif ix == 0:
-                    tile = x_lo[0, iy - 1, iz]
+                if ix == 0:
+                    tile = x_lo[0, iy, iz]
                 elif ix == size_x + 1:
-                    tile = x_hi[0, iy - 1, iz]
-                elif iz < size_z:
-                    tile = own[ix - 1, iy - 1, iz]
+                    tile = x_hi[0, iy, iz]
                 else:
-                    tile = other[ix - 1, iy - 1, iz - size_z]
+                    tile = inner[ix - 1, iy, iz]
                 cell = (ix * (size_y + 2) + iy) * 2 * size_z + iz
-                ext[cell] = tile * scale + shift
+                ext[cell] = tile
                 held = jnp.where(lane == cell, tile, held)
     return held
 
@@ -71,7 +88,7 @@
 
 
 def near_kernel(cells, *refs):
-    pieces, (out_ref, ext, step_ref, count_v, count_s, sem, listed, spread, summed) = refs[:6], refs[6:]
+    pieces, (out_ref, ext, step_ref, count_v, count_s, sem, listed, spread, summed) = refs[:3], refs[3:]
     size_x, size_y, size_z = cells
     n_z = 2 * size_z
     row = lax.broadcasted_iota(jnp.int32, (ROWS, LANES), 0)
@@ -179,24 +196,29 @@
     cells = offsets.shape[1:4]
     slots = offsets.shape[4]
     n_cells = (cells[0] + 2) * (cells[1] + 2) * 2 * cells[2]
-    live = lax.broadcasted_iota(jnp.int32, cells + (slots,), 3) < counts[..., None]
-    spread = jnp.broadcast_to(counts.astype(jnp.float32)[..., None], cells + (slots,))
-    rows = [offsets[i] for i in range(3)] + [jnp.where(live, forces[i], 0.0) for i in range(3)]
-    rows = rows + [spread, jnp.zeros_like(spread)]
-    own = jnp.stack(rows, axis=3)
-
-    size = lax.axis_size("ha")
-    other = lax.ppermute(own, "ha", [(i, (i + 1) % size) for i in range(size)])
-    column = jnp.concatenate([own, other], axis=2)
-    x_lo, x_hi = shifted(column, "gx", 0)
-    wide = jnp.concatenate([x_lo, column, x_hi], axis=0)
-    y_lo, y_hi = shifted(wide, "gy", 1)
-
     whole = pl.BlockSpec(memory_space=pltpu.VMEM)
+    scalars = pl.BlockSpec(memory_space=pltpu.SMEM)
+    own = pl.pallas_call(
+        functools.partial(pack_kernel, cells),
+        out_shape=jax.ShapeDtypeStruct(cells + (ROWS, slots), jnp.float32),
+        in_specs=[scalars, whole, whole],
+        out_specs=whole,
+        name="pack",
+    )(counts, offsets, forces)
+    gathered = lax.all_gather(own, ("gy", "ha"))
+    at = jnp.stack([lax.axis_index("gy"), lax.axis_index("ha")])
+    inner = pl.pallas_call(
+        functools.partial(window_kernel, cells, lax.axis_size("gy") * cells[1]),
+        out_shape=jax.ShapeDtypeStruct((cells[0], cells[1] + 2, 2 * cells[2], ROWS, slots), jnp.float32),
+        in_specs=[scalars, whole],
+        out_specs=whole,
+        name="window",
+    )(at, gathered)
+    x_lo, x_hi = shifted(inner, "gx", 0)
     return pl.pallas_call(
         functools.partial(near_kernel, cells),
         out_shape=jax.ShapeDtypeStruct((3,) + cells + (slots,), jnp.float32),
-        in_specs=[whole] * 6,
+        in_specs=[whole] * 3,
         out_specs=whole,
         scratch_shapes=[
             pltpu.VMEM((n_cells, ROWS, LANES), jnp.float32),
@@ -210,7 +232,7 @@
         ],
         compiler_params=pltpu.CompilerParams(vmem_limit_bytes=16 << 20),
         name="near_field",
-    )(own, other, x_lo, x_hi, y_lo, y_hi)
+    )(inner, x_lo, x_hi)
 
 
 def solution(mesh):

time: 40.3 us -> 52.1 us (1.29)
  blocking collectives: 0 us -> 19.5 us
  waiting for transfers between devices: 11.5 us -> 6.47 us
  starting transfers between devices: 7.69 us -> 3.66 us
  Pallas kernels: 18.9 us -> 20.6 us
  local copies, waits for them, and re-layouts: 1.56 us -> 0.93 us
    all_gather x0 -> x1, blocking collectives: none -> 19.5 us  [on_device(): gathered = lax.all_gather(own, ('gy', 'ha'))]
    ppermute x1 -> x0, starting transfers between devices: 3.03 us -> none  [on_device(): other = lax.ppermute(own, 'ha', [(i, (i + 1) % size) for i in range(size)])]
    pallas_call x0 -> x2, Pallas kernels: none -> 3.01 us  [the longest x1 1.65 us: on_device(): pl.pallas_call(functools.partial(window_kernel, cells, lax.axis_size('gy'...]
    ppermute x2 -> x1, waiting for transfers between devices: 6.64 us -> 4.56 us  [shifted(): lax.ppermute(lax.slice_in_dim(array, length - 1, length, axis=dim), axis,...]
    ppermute x1 -> x0, waiting for transfers between devices: 1.89 us -> none  [on_device(): other = lax.ppermute(own, 'ha', [(i, (i + 1) % size) for i in range(size)])]
    pallas_call x1, Pallas kernels: 18.9 us -> 17.6 us  [on_device(): pl.pallas_call(functools.partial(near_kernel, cells), out_shape=jax.Shape...]
    ppermute x2 -> x1, waiting for transfers between devices: 3 us -> 1.9 us  [shifted(): after = lax.ppermute(lax.slice_in_dim(array, 0, 1, axis=dim), axis, down)]
    slice x1, local copies, waits for them, and re-layouts: 0.01 us -> 0.92 us  [shifted(): after = lax.ppermute(lax.slice_in_dim(array, 0, 1, axis=dim), axis, down)]
  transfers between devices with their start and end apart: 5 -> 2, of which waited for: 5 -> 2; matrix products, arithmetic and copies ran while one was open for 0% -> 0% of each run, Pallas kernels for 0% -> 0%
where the time goes in v2:
time: 52.1 us; the launch traced here: 51.8 us
  Pallas kernels  20.6 us (40%)
  blocking collectives  19.5 us (37%)
  waiting for transfers between devices  6.47 us (12%)
  starting transfers between devices  3.66 us (7%)
  local copies, waits for them, and re-layouts  0.93 us (2%)
  other arithmetic  0.65 us (1%)
    all_gather x1, blocking collectives, on_device(): gathered = lax.all_gather(own, ('gy', 'ha'))  19.5 us
    pallas_call x1, Pallas kernels, on_device(): pl.pallas_call(functools.partial(near_kernel, cells), out_shape=jax.Shape...  17.6 us
    ppermute x1, waiting for transfers between devices, shifted(): lax.ppermute(lax.slice_in_dim(array, length - 1, length, axis=dim), axis,...  4.56 us
    ppermute x1, starting transfers between devices, shifted(): after = lax.ppermute(lax.slice_in_dim(array, 0, 1, axis=dim), axis, down)  3.65 us
    ppermute x1, waiting for transfers between devices, shifted(): after = lax.ppermute(lax.slice_in_dim(array, 0, 1, axis=dim), axis, down)  1.9 us
    pallas_call x1, Pallas kernels, on_device(): pl.pallas_call(functools.partial(window_kernel, cells, lax.axis_size('gy'...  1.65 us
    pallas_call x1, Pallas kernels, on_device(): pl.pallas_call(functools.partial(pack_kernel, cells), out_shape=jax.Shape...  1.37 us
  transfers between devices with their start and end apart: 2, of which 2 were waited for; matrix products, arithmetic and copies ran while one was open for 0% of the time, Pallas kernels for 0%

profile of v2, /device:TPU:0, one launch (start us, length us, event | category | flops | bytes accessed | tf_op | source)
XLA Modules:
  0.0 51.8 jit_solution(16476845993956345630)
XLA Ops:
  0.0 1.4 %pack.1 = f32[2,2,2,8,128]{4,3,2,1,0:T(8,128)} custom-call(s32[2,2,2]{2,1,0:T(2,128)} %count_ref.1, f32[3,2,2,2,128]{4,3,2,1,0:T(2,128)} %offset_ref.1, f32[3,2,2,2,128]{4,3,2,1,0:T(2,128)} %force_ref.1), custom_call_target="tpu_custom_call" | custom-call | tf_op jit(solution)/shard_map/pack/pallas_call | solution.py:201
  1.4 19.5 %all-gather = f32[16,2,2,8,128]{4,3,2,1,0:T(8,128)} all-gather(f32[2,2,2,8,128]{4,3,2,1,0:T(8,128)} %pack.1), channel_id=2, replica_groups=mesh['gx'=4,'gy'=4,'ha'=2] {'gy','ha'}, dimensions={0}, use_global_device_ids=true | all-gather | bytes 294912 | tf_op jit(solution)/shard_map/all_gather | solution.py:208
  20.9 0.6 %pad_add_fusion.at_ref = s32[2]{0:T(128)} fusion(s32[1]{0:T(128)} %bitcast.1, s32[1]{0:T(128)} %bitcast), kind=kLoop, calls=%fused_computation | loop fusion | flops 2 | bytes 16 | tf_op jit(solution)/shard_map/stack | solution.py:209
  21.5 1.6 %window.1.refs_0_ = f32[2,4,4,8,128]{4,3,2,1,0:T(8,128)} custom-call(s32[2]{0:T(128)} %pad_add_fusion.at_ref, f32[8,2,2,2,8,128]{5,4,3,2,1,0:T(8,128)} %bitcast.3), custom_call_target="tpu_custom_call" | custom-call | tf_op jit(solution)/shard_map/window/pallas_call | solution.py:210
  23.2 0.0 copy-start
  23.2 0.9 %fusion = (f32[1,4,4,8,128]{4,3,2,1,0:T(8,128)S(1)}, f32[1,4,4,8,128]{4,3,2,1,0:T(8,128)S(1)}) fusion(f32[2,4,4,8,128]{4,3,2,1,0:T(8,128)} %window.1.refs_0_), kind=kLoop, calls=%fused_computation.1 | loop fusion | bytes 262144 | tf_op jit(solution)/shard_map/slice | solution.py:191
  24.1 3.7 %collective-permute-start.1 = (f32[1,4,4,8,128]{4,3,2,1,0:T(8,128)S(1)}, f32[1,4,4,8,128]{4,3,2,1,0:T(8,128)S(1)}, u32[]{:S(2)}, u32[]{:S(2)}) collective-permute-start(f32[1,4,4,8,128]{4,3,2,1,0:T(8,128)S(1)} %get-tuple-element.5), channel_id=1, source_target_pairs={{8,0},{16,8},{24,16},{0,24},{9,1},{17,9},{25,17},{1,25},{10,2},{18... | collective-permute-start | bytes 196616 | tf_op jit(solution)/shard_map/ppermute | solution.py:191
  27.8 0.0 collective-permute-start
  27.8 1.9 %collective-permute-done.1.refs_2_ = f32[1,4,4,8,128]{4,3,2,1,0:T(8,128)S(1)} collective-permute-done((f32[1,4,4,8,128]{4,3,2,1,0:T(8,128)S(1)}, f32[1,4,4,8,128]{4,3,2,1,0:T(8,128)S(1)}, u32[]{:S(2)}, u32[]{:S(2)}) %collective-permute-start.1) | collective-permute-done | bytes 65568 | tf_op jit(solution)/shard_map/ppermute | solution.py:191
  29.7 4.6 %collective-permute-done.refs_1_ = f32[1,4,4,8,128]{4,3,2,1,0:T(8,128)S(1)} collective-permute-done((f32[1,4,4,8,128]{4,3,2,1,0:T(8,128)S(1)}, f32[1,4,4,8,128]{4,3,2,1,0:T(8,128)S(1)}, u32[]{:S(2)}, u32[]{:S(2)}) %collective-permute-start) | collective-permute-done | bytes 65568 | tf_op jit(solution)/shard_map/ppermute | solution.py:190
  34.2 0.0 copy-done
  34.2 17.6 %near_field.1 = f32[3,2,2,2,128]{4,3,2,1,0:T(2,128)} custom-call(f32[2,4,4,8,128]{4,3,2,1,0:T(8,128)S(1)} %copy-done, f32[1,4,4,8,128]{4,3,2,1,0:T(8,128)S(1)} %collective-permute-done.refs_1_, f32[1,4,4,8,128]{4,3,2,1,0:T(8,128)S(1)} %collective-permute-done.1.refs_2_), custom_call_target="tpu_custom_call" | custom-call | tf_op jit(solution)/shard_map/near_field/pallas_call | solution.py:218
Async XLA Ops:
  23.2 11.1 %copy-start = (f32[2,4,4,8,128]{4,3,2,1,0:T(8,128)S(1)}, f32[2,4,4,8,128]{4,3,2,1,0:T(8,128)}, u32[]{:S(2)}) copy-start(f32[2,4,4,8,128]{4,3,2,1,0:T(8,128)} %window.1.refs_0_) | copy-start | bytes 393220
  24.1 5.6 %collective-permute-start.1 = (f32[1,4,4,8,128]{4,3,2,1,0:T(8,128)S(1)}, f32[1,4,4,8,128]{4,3,2,1,0:T(8,128)S(1)}, u32[]{:S(2)}, u32[]{:S(2)}) collective-permute-start(f32[1,4,4,8,128]{4,3,2,1,0:T(8,128)S(1)} %get-tuple-element.5), channel_id=1, source_target_pairs={{8,0},{16,8},{24,16},{0,24},{9,1},{17,9},{25,17},{1,25},{10,2},{18... | collective-permute-start | bytes 196616 | tf_op jit(solution)/shard_map/ppermute | solution.py:191
  27.8 6.5 %collective-permute-start = (f32[1,4,4,8,128]{4,3,2,1,0:T(8,128)S(1)}, f32[1,4,4,8,128]{4,3,2,1,0:T(8,128)S(1)}, u32[]{:S(2)}, u32[]{:S(2)}) collective-permute-start(f32[1,4,4,8,128]{4,3,2,1,0:T(8,128)S(1)} %get-tuple-element.6), channel_id=1, source_target_pairs={{0,8},{8,16},{16,24},{24,0},{1,9},{9,17},{17,25},{25,1},{2,10},{10... | collective-permute-start | bytes 196616 | tf_op jit(solution)/shard_map/ppermute | solution.py:190
